TPU v7x, 768 devices: a whole 4x8x12 slice. The times are simulated.
768 devices in a mesh: vol: 64 (over x, y, core), seq: 12 (over z).
Axes of the slice: x: 4, y: 8, z: 12, core: 2. Of those that a mesh axis runs over, the one named last changes fastest.
Arguments:
- patches: bfloat16 [64, 3072, 1024], P('vol', 'seq'), may hold values from -6 to 6
- visible: int32 [64, 12, 96], P('vol', 'seq'), may hold values from 0 to 255, as said below
- counts: int32 [64, 12], P('vol'), may hold values from 32 to 96, as said below
- pos_embed: bfloat16 [3072, 512], P('seq'), may hold values from -3 to 3
- mask_token: bfloat16 [512], replicated, may hold values from -4 to 4
- enc_gain: bfloat16 [1024], replicated, may hold values from 0.099609375 to 1.8984375
- enc_qkv: bfloat16 [1024, 2304], P('vol')
- enc_wo: bfloat16 [768, 1024], replicated, may hold values from -1.75 to 1.75
- enc_to_dec: bfloat16 [1024, 512], replicated, may hold values from -0.1875 to 0.1875
- dec_gain: bfloat16 [512], replicated, may hold values from 0.099609375 to 1.8984375
- dec_qkv: bfloat16 [512, 1536], replicated
- dec_wo: bfloat16 [512, 512], replicated, may hold values from -0.25 to 0.25
Outputs:
- decoded: bfloat16 [64, 3072, 512], P('vol', 'seq')
Inputs may be any that keep to these rules, and one draw needn't show every extreme that they name: `counts`: live visible slots of each shard; in every volume some shard has exactly 96. In each shard the first counts entries are the shard's visible token positions in increasing order; the other entries are distinct positions of masked tokens of that shard.
All inputs are finite; a program needn't handle non-finite values.
Results may differ from a plain program's by a relative error of at most 0.014.
Values may be sent and summed in bfloat16 or wider, within the bound.
A program may use at most 64 MiB of HBM per device.

v0:
```python
import math

import jax
import jax.numpy as jnp
from jax import lax
from jax.sharding import PartitionSpec as P

HEADS = 12
DHEADS = 16
LAYER = 128


EPSILON = 1e-06
NEGATIVE = -1e30


def extended(cells, sides, width):
    for axis, dim in sides:
        count = lax.axis_size(axis)
        ends = count - 1
        head = lax.slice_in_dim(cells, 0, width, axis=dim)
        tail = lax.slice_in_dim(cells, cells.shape[dim] - width, cells.shape[dim], axis=dim)
        cells = jnp.concatenate(
            [
                lax.ppermute(tail, axis, [(i, (i + 1) % count) for i in range(ends)]),
                cells,
                lax.ppermute(head, axis, [((i + 1) % count, i) for i in range(ends)]),
            ],
            axis=dim,
        )
    return cells


def layer_norm(values, weights):
    values = values.astype(jnp.float32)
    centred = values - jnp.mean(values, axis=-1, keepdims=True)
    spread = jnp.mean(centred * centred, axis=-1, keepdims=True)
    return centred * lax.rsqrt(spread + EPSILON) * weights.astype(jnp.float32)


def lookup_count(positions, slot_count, count_row):
    owner_index = positions // slot_count
    count_table = jnp.where(
        owner_index[:, None] == jnp.arange(count_row.shape[0], dtype=jnp.int32)[None, :],
        count_row[None, :],
        0,
    )
    return positions % slot_count < jnp.sum(count_table, axis=1)


def local_attend(queries, key_rows, values, key_live, scale):
    scores = (
        jnp.einsum("qhd,khd->hqk", queries, key_rows, preferred_element_type=jnp.float32) * scale
    )
    scores = jnp.where(key_live[None, None, :], scores, NEGATIVE)
    top_seen = jnp.max(scores, axis=-1, keepdims=True)
    raised = jnp.where(key_live[None, None, :], jnp.exp(scores - top_seen), 0.0)
    denom_sum = jnp.sum(raised, axis=-1)
    mixed_rows = jnp.einsum(
        "hqk,khd->qhd", raised.astype(jnp.bfloat16), values, preferred_element_type=jnp.float32
    )
    mixed_rows = mixed_rows / jnp.transpose(denom_sum)[:, :, None]
    return mixed_rows.astype(jnp.bfloat16).reshape(queries.shape[0], -1)


def local(
    patches,
    visible,
    counts,
    pos_embed,
    mask_token,
    enc_gain,
    enc_qkv,
    enc_wo,
    enc_to_dec,
    dec_gain,
    dec_qkv,
    dec_wo,
):
    patch_rows = patches[0]
    vis_rows = visible[0, 0]
    count_row = counts[0]
    slot_count = vis_rows.shape[0]
    tok_dev = patch_rows.shape[0]
    n_seq = lax.axis_size("seq")
    my_index = lax.axis_index("seq")
    attn_width = enc_wo.shape[0]
    head_size = attn_width // HEADS
    enc_scale = 1.0 / math.sqrt(head_size)
    slot_index = jnp.arange(slot_count, dtype=jnp.int32)
    slot_live = lookup_count(my_index * slot_count + slot_index, slot_count, count_row)
    chooser = (vis_rows[:, None] == jnp.arange(tok_dev, dtype=jnp.int32)[None, :]).astype(
        jnp.bfloat16
    )
    x_vis = jnp.dot(chooser, patch_rows, preferred_element_type=jnp.float32).astype(jnp.bfloat16)
    enc_norm = layer_norm(x_vis, enc_gain).astype(jnp.bfloat16)
    enc_proj = jnp.dot(
        enc_norm,
        lax.all_gather(enc_qkv, "vol", axis=0, tiled=True),
        preferred_element_type=jnp.float32,
    ).astype(jnp.bfloat16)
    queries = enc_proj[:, :attn_width].reshape(slot_count, HEADS, head_size)
    shard_rows = lax.all_gather(enc_proj[:, attn_width:], "seq", axis=0, tiled=True)
    top_seen = jnp.full((HEADS, slot_count), NEGATIVE, jnp.float32)
    count_rows = shard_rows.shape[0]
    key_rows = shard_rows[:, :attn_width].reshape(count_rows, HEADS, head_size)
    values = shard_rows[:, attn_width:].reshape(count_rows, HEADS, head_size)
    fold_key_live = lookup_count(jnp.arange(count_rows, dtype=jnp.int32), slot_count, count_row)
    scores = (
        jnp.einsum("qhd,khd->hqk", queries, key_rows, preferred_element_type=jnp.float32)
        * enc_scale
    )
    scores = jnp.where(fold_key_live[None, None, :], scores, NEGATIVE)
    new_top = jnp.maximum(top_seen, jnp.max(scores, axis=-1))
    raised = jnp.where(fold_key_live[None, None, :], jnp.exp(scores - new_top[:, :, None]), 0.0)
    denom_sum = jnp.sum(raised, axis=-1)
    accumulated = jnp.einsum(
        "hqk,khd->hqd", raised.astype(jnp.bfloat16), values, preferred_element_type=jnp.float32
    )
    top_seen, denom_sum, accumulated = (new_top, denom_sum, accumulated)
    enc_mix = (
        jnp.transpose(accumulated / denom_sum[:, :, None], (1, 0, 2))
        .reshape(slot_count, attn_width)
        .astype(jnp.bfloat16)
    )
    enc_out = (
        x_vis.astype(jnp.float32) + jnp.dot(enc_mix, enc_wo, preferred_element_type=jnp.float32)
    ).astype(jnp.bfloat16)
    latent = jnp.dot(enc_out, enc_to_dec, preferred_element_type=jnp.float32).astype(jnp.bfloat16)
    live_chooser = chooser * slot_live[:, None].astype(jnp.bfloat16)
    placed = lax.dot_general(
        live_chooser, latent, (((0,), (0,)), ((), ())), preferred_element_type=jnp.float32
    )
    is_visible = jnp.sum(live_chooser.astype(jnp.float32), axis=0)
    dec_in = jnp.where(
        is_visible[:, None] > 0.5, placed, mask_token.astype(jnp.float32)[None, :]
    ) + pos_embed.astype(jnp.float32)
    dec_width = dec_wo.shape[0]
    dec_head = dec_width // DHEADS
    dec_scale = 1.0 / math.sqrt(dec_head)
    dec_norm = layer_norm(dec_in, dec_gain).astype(jnp.bfloat16)
    dec_proj = jnp.dot(dec_norm, dec_qkv, preferred_element_type=jnp.float32).astype(jnp.bfloat16)
    levels = tok_dev // LAYER
    by_level = dec_proj.reshape(levels, LAYER, 3 * dec_width)
    padded = extended(by_level[:, :, dec_width:], (("seq", 0),), 1)
    global_level = my_index * levels + jnp.arange(levels + 2, dtype=jnp.int32) - 1
    level_live = (global_level >= 0) & (global_level < n_seq * levels)
    level_mix = []
    for z_level in range(levels):
        queries = by_level[z_level, :, :dec_width].reshape(LAYER, DHEADS, dec_head)
        window = padded[z_level : z_level + 3].reshape(3 * LAYER, 2, DHEADS, dec_head)
        key_live = jnp.repeat(level_live[z_level : z_level + 3], LAYER)
        level_mix.append(local_attend(queries, window[:, 0], window[:, 1], key_live, dec_scale))
    dec_mix = jnp.concatenate(level_mix, axis=0)
    decoded = (dec_in + jnp.dot(dec_mix, dec_wo, preferred_element_type=jnp.float32)).astype(
        jnp.bfloat16
    )
    return decoded[None]


def solution(mesh):
    in_specs = (
        P("vol", "seq", None),
        P("vol", "seq", None),
        P("vol", None),
        P("seq", None),
        P(),
        P(),
        P("vol", None),
        P(),
        P(),
        P(),
        P(),
        P(),
    )
    out_specs = P("vol", "seq", None)
    return jax.shard_map(local, mesh=mesh, in_specs=in_specs, out_specs=out_specs, check_vma=False)
```

profile of v0, /device:TPU:6, one launch (start us, length us, event | category | flops | bytes accessed | tf_op | source)
XLA Modules:
  0.0 241.7 jit_solution(669169924658245041)
XLA Ops:
  8.0 1.4 fusion.91
  9.7 97.0 %all-gather.3.cloned.1.call-done = bf16[1024,2304]{1,0:T(8,128)(2,1)} async-done(((bf16[16,2304]{1,0:T(8,128)(2,1)}), bf16[1024,2304]{1,0:T(8,128)(2,1)}) %all-gather.3.cloned.1.call-update) | async-done | bytes 4718608 | tf_op jit(solution)/shard_map/all_gather | solution.py:99
  106.7 3.3 %convolution_convert_fusion = bf16[96,2304]{1,0:T(8,128)(2,1)S(1)} fusion(bf16[1024,2304]{1,0:T(8,128)(2,1)} %all-gather.3.cloned.1.call-done, f32[96,1024]{1,0:T(8,128)S(1)} %get-tuple-element.16, f32[1024]{0:T(1024)S(1)} %convert_element_type.77, f32[96]{0:T(128)S(1)} %add_rsqrt_fusion.1, f32[96]{0:T(128)S(1)} %broadcast_multiply_fusion.1), kind=kOutput, calls=%fused_computation.6 | convolution fusion | flops 453599232 | bytes 5559040 | tf_op jit(solution)/shard_map/dot_general | solution.py:97
  113.1 61.8 %all-gather.5.cloned.1.call-done = bf16[1152,1536]{1,0:T(8,128)(2,1)} async-done(((bf16[96,1536]{1,0:T(8,128)(2,1)}), bf16[1152,1536]{1,0:T(8,128)(2,1)}) %all-gather.5.cloned.1.call-update) | async-done | bytes 3538960 | tf_op jit(solution)/shard_map/all_gather | solution.py:103
  174.9 3.5 %fusion.87 = (bf16[1152,768]{1,0:T(8,128)(2,1)}, bf16[1152,768]{1,0:T(8,128)(2,1)S(1)}) fusion(bf16[1152,1536]{1,0:T(8,128)(2,1)} %all-gather.5.cloned.1.call-done), kind=kLoop, calls=%fused_computation.113 | loop fusion | bytes 7077888 | tf_op jit(solution)/shard_map/slice | solution.py:106
  178.3 3.9 %copy.29 = bf16[1152,768]{0,1:T(8,128)(2,1)} copy(bf16[1152,768]{1,0:T(8,128)(2,1)} %get-tuple-element.5) | data formatting | bytes 3538944 | tf_op jit(solution)/shard_map/slice | solution.py:106
  182.2 4.7 %fusion.92 = (f32[12,96]{1,0:T(8,128)S(1)}, f32[12,96,1152]{2,1,0:T(8,128)}) fusion(bf16[96,12,64]{0,2,1:T(8,128)(2,1)S(1)} %bitcast.78, bf16[1152,12,64]{0,2,1:T(8,128)(2,1)} %bitcast.73, pred[1152]{0:T(1024)(128)(4,1)S(1)} %fusion.73), kind=kOutput, calls=%fused_computation.118 | convolution fusion | flops 173849472 | bytes 7231104 | tf_op jit(solution)/shard_map/qhd,khd->hqk/dot_general | solution.py:110
  186.9 2.2 copy.30
  189.2 3.8 %fusion.2 = f32[12,96]{1,0:T(8,128)S(1)} fusion(f32[12,96,1152]{2,1,0:T(8,128)} %get-tuple-element.18, f32[12,96]{1,0:T(8,128)S(1)} %broadcast_maximum_fusion, pred[1152]{0:T(1024)(128)(4,1)S(1)} %fusion.73), kind=kLoop, calls=%fused_computation.4 | loop fusion | flops 3980160 | bytes 5318784 | tf_op jit(solution)/shard_map/reduce_sum | solution.py:116
  193.2 3.6 %fusion.52 = bf16[96,12,64]{0,2,1:T(8,128)(2,1)} fusion(bf16[1152,12,64]{0,2,1:T(8,128)(2,1)} %bitcast.77, f32[12,96,1152]{2,1,0:T(8,128)S(1)} %copy-done.1, f32[12,96]{1,0:T(8,128)S(1)} %broadcast_maximum_fusion, pred[1152]{0:T(1024)(128)(4,1)S(1)} %fusion.73, f32[96,12]{0,1:T(8,128)S(1)} %bitcast.84), kind=kOutput, calls=%fused_computation.49 | convolution fusion | flops 173998080 | bytes 7235712 | tf_op jit(solution)/shard_map/hqk,khd->hqd/dot_general | solution.py:117
  196.9 2.6 %fusion.48 = bf16[96,512]{1,0:T(8,128)(2,1)} fusion(bf16[1024,512]{1,0:T(8,128)(2,1)} %param.20, f32[96,1024]{1,0:T(8,128)S(1)} %copy-done.3, bf16[96,768]{0,1:T(8,128)(2,1)} %bitcast.81, bf16[768,1024]{1,0:T(8,128)(2,1)S(1)} %copy-done.6), kind=kOutput, calls=%fused_computation.45 | convolution fusion | flops 251904000 | bytes 3260416 | tf_op jit(solution)/shard_map/dot_general | solution.py:129
  199.4 1.4 fusion.93
  202.9 3.2 %collective-permute-start = (bf16[1,128,1024]{1,0,2:T(2,128)(2,1)}, bf16[1,128,1024]{1,0,2:T(2,128)(2,1)}, u32[]{:S(2)}, u32[]{:S(2)}) collective-permute-start(bf16[1,128,1024]{1,0,2:T(2,128)(2,1)} %copy.36), channel_id=1, source_target_pairs={{0,1},{1,2},{2,3},{3,4},{4,5},{5,6},{6,7},{7,8},{8,9},{9,10},{10,1... | collective-permute-start | bytes 786440 | tf_op jit(solution)/shard_map/ppermute | solution.py:25
  206.1 1.1 copy.38
  207.2 1.5 collective-permute-start.1
  208.8 1.1 copy.37
  210.2 2.1 collective-permute-done
  212.3 6.3 %collective-permute-done.1 = bf16[1,128,1024]{1,0,2:T(2,128)(2,1)} collective-permute-done((bf16[1,128,1024]{1,0,2:T(2,128)(2,1)}, bf16[1,128,1024]{1,0,2:T(2,128)(2,1)}, u32[]{:S(2)}, u32[]{:S(2)}) %collective-permute-start.1) | collective-permute-done | bytes 262176 | tf_op jit(solution)/shard_map/ppermute | solution.py:27
  218.6 4.2 %pad_maximum_fusion = (bf16[3,128,1024]{1,0,2:T(4,128)(2,1)}, bf16[3,128,1024]{1,0,2:T(4,128)(2,1)S(1)}) fusion(bf16[2,128,1024]{1,0,2:T(2,128)(2,1)} %copy.37, bf16[1,128,1024]{1,0,2:T(2,128)(2,1)} %collective-permute-done, bf16[1,128,1024]{1,0,2:T(2,128)(2,1)} %collective-permute-done.1), kind=kLoop, calls=%fused_computation.46 | loop fusion | flops 3145728 | bytes 2621440 | tf_op jit(solution)/shard_map/concatenate | solution.py:23
  222.7 3.2 %reshape.120 = bf16[384,2,16,32]{0,3,2,1:T(8,128)(2,1)} reshape(bf16[3,128,1024]{1,0,2:T(4,128)(2,1)} %get-tuple-element.11) | data formatting | bytes 1572864 | tf_op jit(solution)/shard_map/reshape | solution.py:151
  226.0 1.4 reshape.122
  227.4 1.6 fusion.57
  229.0 1.4 fusion.95
  231.8 1.4 fusion.94
  (73 shorter events, 10.3 us)
Async XLA Ops:
  6.5 194.6 %copy-start = (bf16[512,1536]{1,0:T(8,128)(2,1)S(1)}, bf16[512,1536]{1,0:T(8,128)(2,1)}, u32[]{:S(2)}) copy-start(bf16[512,1536]{1,0:T(8,128)(2,1)} %param.22) | copy-start | bytes 4718596
  6.5 100.2 %all-gather.3.cloned.1.call-start = ((), (), s32[]{:S(2)}) async-start(), calls=%async_computation | async-start | bytes 4792320 | tf_op jit(solution)/shard_map/all_gather | solution.py:99
  7.3 167.6 %all-gather.5.cloned.1.call-start = ((), (), s32[]{:S(2)}) async-start(), calls=%async_computation.1 | async-start | bytes 3833856 | tf_op jit(solution)/shard_map/all_gather | solution.py:103
  9.4 101.3 %copy-start.2 = (f32[96,1024]{1,0:T(8,128)}, f32[96,1024]{1,0:T(8,128)S(1)}, u32[]{:S(2)}) copy-start(f32[96,1024]{1,0:T(8,128)S(1)} %get-tuple-element.16) | copy-start | bytes 1179652
  9.6 101.1 %copy-start.14 = (bf16[512]{0:T(512)(128)(2,1)S(1)}, bf16[512]{0:T(512)(128)(2,1)}, u32[]{:S(2)}) copy-start(bf16[512]{0:T(512)(128)(2,1)} %param.16) | copy-start | bytes 3076
  9.7 101.1 %copy-start.15 = (bf16[512]{0:T(512)(128)(2,1)S(1)}, bf16[512]{0:T(512)(128)(2,1)}, u32[]{:S(2)}) copy-start(bf16[512]{0:T(512)(128)(2,1)} %param.21) | copy-start | bytes 3076
  9.7 101.8 %copy-start.16 = (s32[1,12]{1,0:T(1,128)S(1)}, s32[1,12]{1,0:T(1,128)}, u32[]{:S(2)}) copy-start(s32[1,12]{1,0:T(1,128)} %param.14) | copy-start | bytes 148
  9.7 102.0 %copy-start.9 = (s32[1,1,96]{2,1,0:T(1,128)S(1)}, s32[1,1,96]{2,1,0:T(1,128)}, u32[]{:S(2)}) copy-start(s32[1,1,96]{2,1,0:T(1,128)} %param.13) | copy-start | bytes 1156
  111.6 1.5 copy-start.11
  189.2 4.1 %copy-start.1 = (f32[12,96,1152]{2,1,0:T(8,128)S(1)}, f32[12,96,1152]{2,1,0:T(8,128)}, u32[]{:S(2)}) copy-start(f32[12,96,1152]{2,1,0:T(8,128)} %get-tuple-element.18) | copy-start | bytes 15925252
  193.2 3.6 %copy-start.3 = (f32[96,1024]{1,0:T(8,128)S(1)}, f32[96,1024]{1,0:T(8,128)}, u32[]{:S(2)}) copy-start(f32[96,1024]{1,0:T(8,128)} %copy-done.2) | copy-start | bytes 1179652
  193.2 3.6 %copy-start.6 = (bf16[768,1024]{1,0:T(8,128)(2,1)S(1)}, bf16[768,1024]{1,0:T(8,128)(2,1)}, u32[]{:S(2)}) copy-start(bf16[768,1024]{1,0:T(8,128)(2,1)} %param.19) | copy-start | bytes 4718596
  196.8 2.6 %copy-start.10 = (s32[1,1,96]{2,1,0:T(1,128)S(1)}, s32[1,1,96]{2,1,0:T(1,128)}, u32[]{:S(2)}) copy-start(s32[1,1,96]{2,1,0:T(1,128)} %param.13) | copy-start | bytes 1156
  196.8 4.3 %copy-start.8 = (f32[512]{0:T(512)S(1)}, f32[512]{0:T(512)}, u32[]{:S(2)}) copy-start(f32[512]{0:T(512)} %convert_element_type.87) | copy-start | bytes 6148
  200.9 7.8 %copy-start.12 = (pred[3]{0:T(512)(128)(4,1)S(1)}, pred[3]{0:T(512)(128)(4,1)}, u32[]{:S(2)}) copy-start(pred[3]{0:T(512)(128)(4,1)} %get-tuple-element.13) | copy-start | bytes 13
  200.9 7.8 %copy-start.13 = (pred[3]{0:T(512)(128)(4,1)S(1)}, pred[3]{0:T(512)(128)(4,1)}, u32[]{:S(2)}) copy-start(pred[3]{0:T(512)(128)(4,1)} %get-tuple-element.14) | copy-start | bytes 13
  202.9 9.3 %collective-permute-start = (bf16[1,128,1024]{1,0,2:T(2,128)(2,1)}, bf16[1,128,1024]{1,0,2:T(2,128)(2,1)}, u32[]{:S(2)}, u32[]{:S(2)}) collective-permute-start(bf16[1,128,1024]{1,0,2:T(2,128)(2,1)} %copy.36), channel_id=1, source_target_pairs={{0,1},{1,2},{2,3},{3,4},{4,5},{5,6},{6,7},{7,8},{8,9},{9,10},{10,1... | collective-permute-start | bytes 786440 | tf_op jit(solution)/shard_map/ppermute | solution.py:25
  207.2 11.4 %collective-permute-start.1 = (bf16[1,128,1024]{1,0,2:T(2,128)(2,1)}, bf16[1,128,1024]{1,0,2:T(2,128)(2,1)}, u32[]{:S(2)}, u32[]{:S(2)}) collective-permute-start(bf16[1,128,1024]{1,0,2:T(2,128)(2,1)} %copy.38), channel_id=1, source_target_pairs={{1,0},{2,1},{3,2},{4,3},{5,4},{6,5},{7,6},{8,7},{9,8},{10,9},{11,1... | collective-permute-start | bytes 786440 | tf_op jit(solution)/shard_map/ppermute | solution.py:27
  229.0 1.4 copy-start.5
  229.0 2.1 copy-start.4
  231.8 2.1 copy-start.7
Sparse Core Ops, SparseCore 0:
  11.3 95.3 all-gather.2
  110.9 63.9 all-gather.4
where the time goes:
time: 242 us
  waiting for transfers between devices  168 us (69%)
  matrix products  22.2 us (9%)
  local copies, waits for them, and re-layouts  19.9 us (8%)
  between operations  13.8 us (6%)
  other arithmetic  13.3 us (5%)
  starting transfers between devices  4.66 us (2%)
    all_gather x1, waiting for transfers between devices, local(): lax.all_gather(enc_qkv, 'vol', axis=0, tiled=True)  97 us
    all_gather x1, waiting for transfers between devices, local(): lax.all_gather(enc_proj[:, attn_width:], 'seq', axis=0, tiled=True)  61.8 us
    slice x2, local copies, waits for them, and re-layouts, local(): key_rows = shard_rows[:, :attn_width].reshape(count_rows, HEADS, head_size)  7.34 us
    ppermute x1, waiting for transfers between devices, extended(): lax.ppermute(head, axis, [((i + 1) % count, i) for i in range(ends)])  6.29 us
  transfers between devices with their start and end apart: 4, of which 4 were waited for; matrix products, arithmetic and copies ran while one was open for 3% of the time, Pallas kernels for 0%

commit v1 on v0

v1 whole, which is shorter than its diff:
```python
import functools
import math

import jax
import jax.numpy as jnp
from jax import lax
from jax.experimental import pallas as pl
from jax.experimental.pallas import tpu as pltpu
from jax.sharding import PartitionSpec as P

MESH = pl.DeviceIdType.MESH
BF = jnp.bfloat16
F32 = jnp.float32

HEADS = 12
DHEADS = 16
NX, NY, NC, NZ = 4, 8, 2, 12
CAP = 96
TOK = 256
LAYER = 128
D = 1024
HA = 768
HG = HA // 2
WG = 3 * HG
DD = 512
ROWS = 16
HALF = CAP // 2
EPSILON = 1e-06
NEGATIVE = -1e30
OWN = 4
FIRST = 9
LOG2E = math.log2(math.e)


def dot(a, b):
    return jnp.dot(a, b, preferred_element_type=F32)


def dot_nt(a, b):
    return lax.dot_general(a, b, (((1,), (1,)), ((), ())), preferred_element_type=F32)


def layer_norm(values, weights):
    centred = values - jnp.mean(values, axis=-1, keepdims=True)
    spread = jnp.mean(centred * centred, axis=-1, keepdims=True)
    return centred * lax.rsqrt(spread + EPSILON) * weights


def slot_r(k):
    return (OWN - k) % NZ


def slot_l(k):
    return (OWN + k) % NZ


def kernel(
    patches,
    visible,
    counts,
    pos_embed,
    mask_token,
    enc_gain,
    enc_qkv,
    enc_wo,
    enc_to_dec,
    dec_gain,
    dec_qkv,
    dec_wo,
    out,
    patch_v,
    pos_v,
    wo_v,
    e2d_v,
    dqkv_v,
    dwo_v,
    w_all,
    x_all,
    x_own,
    kv_all,
    q_all,
    o_first,
    m_first,
    l_first,
    mix_own,
    mix_send,
    mix_recv,
    dn_all,
    dec_in,
    dkv,
    dmix,
    load_sem,
    zs,
    zr,
    ws,
    wr,
    cs,
    cr,
    rs,
    rr,
    hs,
    hr,
):
    v = lax.axis_index("vol")
    z = lax.axis_index("seq")
    core = v % NC
    y = (v // NC) % NY
    x = v // (NC * NY)
    part = z % 2

    def vol_of(px, py, pc):
        return (px * NY + py) * NC + pc

    right = (v, (z + 1) % NZ)
    left = (v, (z + NZ - 1) % NZ)
    mate = (v, z + 1 - 2 * part)
    up = (vol_of(x, (y + 1) % NY, core), z)
    down = (vol_of(x, (y + NY - 1) % NY, core), z)
    sibling = (vol_of(x, y, 1 - core), z)
    x_dev = [(vol_of((x + i) % NX, y, core), z) for i in range(NX)]

    barrier = pltpu.get_barrier_semaphore()
    partners = [right, left, up, down, sibling] + x_dev[1:]
    for device in partners:
        pl.semaphore_signal(barrier, inc=1, device_id=device, device_id_type=MESH)

    loads = {}

    def load(name, src, dst, index):
        copy = pltpu.make_async_copy(src, dst, load_sem.at[index])
        copy.start()
        loads[name] = copy

    for i in range(3):
        column = pl.multiple_of(i * HA + part * HG, 128)
        load(
            "w%d" % i,
            enc_qkv.at[:, pl.ds(column, HG)],
            w_all.at[x, y, core, :, pl.ds(i * HG, HG)],
            i,
        )
    load("patches", patches, patch_v, 3)
    load("pos", pos_embed, pos_v, 4)
    load("wo", enc_wo, wo_v, 5)
    load("e2d", enc_to_dec, e2d_v, 6)
    load("dqkv", dec_qkv, dqkv_v, 7)
    load("dwo", dec_wo, dwo_v, 8)

    sends = []

    def remote(src, dst, send_sem, recv_sem, device):
        copy = pltpu.make_async_remote_copy(
            src_ref=src,
            dst_ref=dst,
            send_sem=send_sem,
            recv_sem=recv_sem,
            device_id=device,
            device_id_type=MESH,
        )
        return copy

    def start(copy):
        copy.start()
        sends.append(copy)

    def z_copy(k, h, to_right):
        rows = pl.ds(h * HALF, HALF)
        slot = slot_r if to_right else slot_l
        side = 0 if to_right else 1
        index = ((k - 1) * 2 + h) * 2 + side
        return remote(
            x_all.at[slot(k - 1), rows],
            x_all.at[slot(k), rows],
            zs.at[index],
            zr.at[index],
            right if to_right else left,
        )

    def z_has(k, h, to_right):
        return k < 6 or (k == 6 and (h == 0) == to_right)

    def z_event(k, h):
        for to_right in (True, False):
            if z_has(k, h, to_right):
                z_copy(k, h, to_right).wait_recv()
                if z_has(k + 1, h, to_right):
                    start(z_copy(k + 1, h, to_right))

    def wx_copy(i, other):
        cell = w_all.at[other, y, core]
        return remote(cell, cell, ws.at[i - 1], wr.at[i - 1], x_dev[i])

    def wy_copy(j, h, upward):
        owner = (y + NY - (j - 1)) % NY if upward else (y + j - 1) % NY
        cell = w_all.at[pl.ds(h * 2, 2), owner, core]
        index = NX - 1 + ((j - 1) * 2 + h) * 2 + (0 if upward else 1)
        return remote(cell, cell, ws.at[index], wr.at[index], up if upward else down)

    def wy_has(j, h, upward):
        return j < 4 or (j == 4 and (h == 0) == upward)

    def wy_recv(j, h, upward):
        owner = (y + NY - j) % NY if upward else (y + j) % NY
        cell = w_all.at[pl.ds(h * 2, 2), owner, core]
        index = NX - 1 + ((j - 1) * 2 + h) * 2 + (0 if upward else 1)
        remote(cell, cell, ws.at[index], wr.at[index], up if upward else down).wait_recv()

    def wc_copy(offset, of_core):
        cell = w_all.at[:, (y + offset) % NY, of_core]
        return remote(cell, cell, cs.at[offset], cr.at[offset], sibling)

    def wx_event():
        for i in range(1, NX):
            cell = w_all.at[(x + NX - i) % NX, y, core]
            remote(cell, cell, ws.at[i - 1], wr.at[i - 1], x_dev[i]).wait_recv()
        for h in range(2):
            for upward in (True, False):
                start(wy_copy(1, h, upward))
        start(wc_copy(0, core))

    def wy_event(j, h):
        for upward in (True, False):
            if wy_has(j, h, upward):
                wy_recv(j, h, upward)
                if wy_has(j + 1, h, upward):
                    start(wy_copy(j + 1, h, upward))
        if h == 1:
            start(wc_copy(j, core))
            if j < 4:
                start(wc_copy(NY - j, core))

    for i in range(3):
        loads["w%d" % i].wait()
    pl.semaphore_wait(barrier, len(partners))
    for i in range(1, NX):
        start(wx_copy(i, x))

    loads["patches"].wait()
    token = lax.broadcasted_iota(jnp.int32, (TOK, CAP), 0)
    slot = lax.broadcasted_iota(jnp.int32, (TOK, CAP), 1)
    chooser = visible[...] == token
    chosen = jnp.where(chooser, 1.0, 0.0)
    x_vis = dot(jnp.transpose(chosen).astype(BF), patch_v[...])
    x_own[...] = x_vis
    normed = layer_norm(x_vis, enc_gain[...].astype(F32)).astype(BF)
    x_all[OWN] = normed
    for h in range(2):
        for to_right in (True, False):
            start(z_copy(1, h, to_right))

    count = counts[0, z]
    live_chosen = jnp.where(chooser & (slot < count), 1.0, 0.0)
    is_visible = jnp.sum(live_chosen, axis=1, keepdims=True) > 0.5

    key_index = lax.broadcasted_iota(jnp.int32, (1, NZ * CAP), 1)
    limit = jnp.zeros((1, NZ * CAP), jnp.int32)
    for e in range(NZ):
        limit = jnp.where(
            key_index >= e * CAP, e * CAP + counts[0, (z + e + NZ - OWN) % NZ], limit
        )
    bias = jnp.where(key_index < limit, 0.0, NEGATIVE)

    wx_event()
    z_event(1, 0)
    wy_event(1, 0)
    wy_event(1, 1)
    z_event(1, 1)
    wy_event(2, 0)
    z_event(2, 0)
    wy_event(2, 1)
    wy_event(3, 0)
    z_event(2, 1)
    wy_event(3, 1)
    z_event(3, 0)
    wy_event(4, 0)
    wy_event(4, 1)
    for offset in range(NY):
        wc_copy(offset, 1 - core).wait_recv()
    z_event(3, 1)

    weights = w_all.reshape(D, WG)

    def project(first, last):
        rows = x_all[first:last].reshape((last - first) * CAP, D)
        kv_all[first * CAP : last * CAP, :] = dot(rows, weights[:, HG:]).astype(BF)

    lane = lax.broadcasted_iota(jnp.int32, (2 * CAP, 128), 1) // 64

    mate_slot = OWN + 1 - 2 * part
    pair = jnp.concatenate([x_all[mate_slot], x_all[OWN]], axis=0)
    q_all[...] = (dot(pair, weights[:, :HG]).astype(BF) * 0.125).astype(BF)
    project(1, 8)
    z_event(4, 0)
    z_event(4, 1)
    project(0, 1)
    project(8, 9)

    def attend(pair_index, first, last):
        cols = slice(pair_index * 128, (pair_index + 1) * 128)
        queries = q_all[:, cols]
        keys = kv_all[first * CAP : last * CAP, cols]
        values = kv_all[first * CAP : last * CAP, HG + pair_index * 128 : HG + (pair_index + 1) * 128]
        row_bias = bias[:, first * CAP : last * CAP]
        parts = []
        for s in range(2):
            one = jnp.where(lane == s, queries, jnp.zeros_like(queries))
            scores = dot_nt(one, keys) + row_bias
            top = jnp.max(scores, axis=-1, keepdims=True)
            raised = jnp.exp(scores - top)
            total = jnp.sum(raised, axis=-1, keepdims=True)
            parts.append((top, total, dot(raised.astype(BF), values)))
        (t0, l0, o0), (t1, l1, o1) = parts
        return (
            jnp.where(lane == 0, t0, t1),
            jnp.where(lane == 0, l0, l1),
            jnp.where(lane == 0, o0, o1),
        )

    def first_part(p):
        cols = slice(p * 128, (p + 1) * 128)
        top, total, mixed = attend(p, 0, FIRST)
        m_first[:, cols] = top
        l_first[:, cols] = total
        o_first[:, cols] = mixed

    first_part(0)
    z_event(5, 0)
    first_part(1)
    z_event(5, 1)
    first_part(2)
    z_event(6, 0)
    z_event(6, 1)
    project(FIRST, NZ)
    for p in range(3):
        cols = slice(p * 128, (p + 1) * 128)
        top, total, mixed = attend(p, FIRST, NZ)
        old = m_first[:, cols]
        new = jnp.maximum(old, top)
        a, b = jnp.exp(old - new), jnp.exp(top - new)
        mixed = o_first[:, cols] * a + mixed * b
        total = l_first[:, cols] * a + total * b
        mixed = (mixed / total).astype(BF)
        mix_send[:, cols] = mixed[:CAP]
        mix_own[:, cols] = mixed[CAP:]

    back = remote(mix_send, mix_recv, rs, rr, mate)
    start(back)
    loads["wo"].wait()
    own_rows = pl.multiple_of(part * HG, 128)
    mate_rows = pl.multiple_of((1 - part) * HG, 128)
    enc_out = x_own[...] + dot(mix_own[...], wo_v[pl.ds(own_rows, HG), :])
    loads["e2d"].wait()
    loads["pos"].wait()
    loads["dqkv"].wait()
    loads["dwo"].wait()
    back.wait_recv()
    enc_out = enc_out + dot(mix_recv[...], wo_v[pl.ds(mate_rows, HG), :])
    latent = dot(enc_out.astype(BF), e2d_v[...]).astype(BF)
    placed = dot(live_chosen.astype(BF), latent)
    dec = jnp.where(is_visible, placed, mask_token[...].astype(F32)) + pos_v[...].astype(F32)
    dec_in[...] = dec
    dnorm = layer_norm(dec, dec_gain[...].astype(F32)).astype(BF)
    dn_all[1] = dnorm[:LAYER]
    dn_all[2] = dnorm[LAYER:]
    halo_r = remote(dn_all.at[2], dn_all.at[0], hs.at[0], hr.at[0], right)
    halo_l = remote(dn_all.at[1], dn_all.at[3], hs.at[1], hr.at[1], left)
    start(halo_r)
    start(halo_l)

    proj = dot(dnorm, dqkv_v[...]).astype(BF)
    dq = proj[:, :DD]
    dkv[LAYER : LAYER + TOK, :] = proj[:, DD:]
    scale = LOG2E / math.sqrt(DD // DHEADS)
    quad_lane = lax.broadcasted_iota(jnp.int32, (TOK, 128), 1) // 32

    def quad(queries, keys, values, row_bias, lanes):
        top = total = mixed = None
        for s in range(4):
            one = jnp.where(lanes == s, queries, jnp.zeros_like(queries))
            scores = dot_nt(one, keys) * scale
            if row_bias is not None:
                scores = scores + row_bias
            t = jnp.max(scores, axis=-1, keepdims=True)
            raised = jnp.exp2(scores - t)
            l = jnp.sum(raised, axis=-1, keepdims=True)
            o = dot(raised.astype(BF), values)
            if s == 0:
                top = jnp.broadcast_to(t, o.shape)
                total = jnp.broadcast_to(l, o.shape)
                mixed = o
            else:
                top = jnp.where(lanes == s, t, top)
                total = jnp.where(lanes == s, l, total)
                mixed = jnp.where(lanes == s, o, mixed)
        return top, total, mixed

    local = []
    for g in range(4):
        cols = slice(g * 128, (g + 1) * 128)
        local.append(
            quad(
                dq[:, cols],
                dkv[LAYER : LAYER + TOK, cols],
                dkv[LAYER : LAYER + TOK, DD + g * 128 : DD + (g + 1) * 128],
                None,
                quad_lane,
            )
        )

    halo_r.wait_recv()
    halo_l.wait_recv()
    dkv[:LAYER, :] = dot(dn_all[0], dqkv_v[:, DD:]).astype(BF)
    dkv[LAYER + TOK :, :] = dot(dn_all[3], dqkv_v[:, DD:]).astype(BF)
    low_bias = jnp.where(z == 0, NEGATIVE, 0.0)
    high_bias = jnp.where(z == NZ - 1, NEGATIVE, 0.0)
    half_lane = quad_lane[:LAYER]
    for g in range(4):
        cols = slice(g * 128, (g + 1) * 128)
        value_cols = slice(DD + g * 128, DD + (g + 1) * 128)
        for level in range(2):
            rows = slice(level * LAYER, (level + 1) * LAYER)
            key_rows = slice(0, LAYER) if level == 0 else slice(LAYER + TOK, 2 * LAYER + TOK)
            top, total, mixed = quad(
                dq[rows, cols],
                dkv[key_rows, cols],
                dkv[key_rows, value_cols],
                low_bias if level == 0 else high_bias,
                half_lane,
            )
            old = local[g][0][rows]
            new = jnp.maximum(old, top)
            a, b = jnp.exp2(old - new), jnp.exp2(top - new)
            mixed = local[g][2][rows] * a + mixed * b
            total = local[g][1][rows] * a + total * b
            dmix[rows, cols] = (mixed / total).astype(BF)
    out[...] = (dec_in[...] + dot(dmix[...], dwo_v[...])).astype(BF)

    for copy in sends:
        copy.wait_send()


def local(
    patches,
    visible,
    counts,
    pos_embed,
    mask_token,
    enc_gain,
    enc_qkv,
    enc_wo,
    enc_to_dec,
    dec_gain,
    dec_qkv,
    dec_wo,
):
    vm = pl.BlockSpec(memory_space=pltpu.VMEM)
    sm = pl.BlockSpec(memory_space=pltpu.SMEM)
    hbm = pl.BlockSpec(memory_space=pl.ANY)
    dma = pltpu.SemaphoreType.DMA
    decoded = pl.pallas_call(
        kernel,
        out_shape=jax.ShapeDtypeStruct((TOK, DD), BF),
        in_specs=[hbm, vm, sm, hbm, vm, vm, hbm, hbm, hbm, vm, hbm, hbm],
        out_specs=vm,
        scratch_shapes=[
            pltpu.VMEM((TOK, D), BF),
            pltpu.VMEM((TOK, DD), BF),
            pltpu.VMEM((HA, D), BF),
            pltpu.VMEM((D, DD), BF),
            pltpu.VMEM((DD, 3 * DD), BF),
            pltpu.VMEM((DD, DD), BF),
            pltpu.VMEM((NX, NY, NC, ROWS, WG), BF),
            pltpu.VMEM((NZ, CAP, D), BF),
            pltpu.VMEM((CAP, D), F32),
            pltpu.VMEM((NZ * CAP, 2 * HG), BF),
            pltpu.VMEM((2 * CAP, HG), BF),
            pltpu.VMEM((2 * CAP, HG), F32),
            pltpu.VMEM((2 * CAP, HG), F32),
            pltpu.VMEM((2 * CAP, HG), F32),
            pltpu.VMEM((CAP, HG), BF),
            pltpu.VMEM((CAP, HG), BF),
            pltpu.VMEM((CAP, HG), BF),
            pltpu.VMEM((4, LAYER, DD), BF),
            pltpu.VMEM((TOK, DD), F32),
            pltpu.VMEM((2 * LAYER + TOK, 2 * DD), BF),
            pltpu.VMEM((TOK, DD), BF),
            dma((9,)),
            dma((24,)),
            dma((24,)),
            dma((NX - 1 + 16,)),
            dma((NX - 1 + 16,)),
            dma((NY,)),
            dma((NY,)),
            dma,
            dma,
            dma((2,)),
            dma((2,)),
        ],
        compiler_params=pltpu.CompilerParams(
            collective_id=0, has_side_effects=True, vmem_limit_bytes=48 * 2**20
        ),
        cost_estimate=pl.CostEstimate(
            flops=3 * 10**9, bytes_accessed=10 * 2**20, transcendentals=3 * 10**6
        ),
        name="volume",
    )(
        patches[0],
        visible[0],
        counts,
        pos_embed,
        mask_token[None],
        enc_gain[None],
        enc_qkv,
        enc_wo,
        enc_to_dec,
        dec_gain[None],
        dec_qkv,
        dec_wo,
    )
    return decoded[None]


def solution(mesh):
    in_specs = (
        P("vol", "seq", None),
        P("vol", "seq", None),
        P("vol", None),
        P("seq", None),
        P(),
        P(),
        P("vol", None),
        P(),
        P(),
        P(),
        P(),
        P(),
    )
    out_specs = P("vol", "seq", None)
    return jax.shard_map(local, mesh=mesh, in_specs=in_specs, out_specs=out_specs, check_vma=False)
```

time: 242 us -> 85.3 us (0.35)
  the two profiles are of different devices: /device:TPU:6 before, /device:TPU:8 now
where the time goes in v1:
time: 85.3 us; the launch traced here: 84.8 us
  Pallas kernels  72.8 us (85%)
  local copies, waits for them, and re-layouts  12 us (14%)
    pallas_call x1, Pallas kernels, local(): pl.pallas_call(kernel, out_shape=jax.ShapeDtypeStruct((TOK, DD), BF), in_...  72.8 us
    unnamed x19, local copies, waits for them, and re-layouts  9.97 us

profile of v1, /device:TPU:8, one launch (start us, length us, event | category | flops | bytes accessed | tf_op | source)
XLA Modules:
  0.0 84.8 jit_solution(17916607785784414320)
XLA Ops:
  0.0 0.7 broadcast_in_dim.12.mask_token
  0.7 0.7 broadcast_in_dim.14.dec_gain
  1.4 0.7 broadcast_in_dim.13.enc_gain
  2.1 0.0 copy-start
  2.1 1.4 %copy-done = bf16[768,1024]{1,0:T(8,128)(2,1)S(1)} copy-done((bf16[768,1024]{1,0:T(8,128)(2,1)S(1)}, bf16[768,1024]{1,0:T(8,128)(2,1)}, u32[]{:S(2)}) %copy-start) | copy-done | bytes 1572888
  3.5 0.0 copy-start.1
  3.5 1.4 %copy-done.1 = bf16[512,1536]{1,0:T(8,128)(2,1)S(1)} copy-done((bf16[512,1536]{1,0:T(8,128)(2,1)S(1)}, bf16[512,1536]{1,0:T(8,128)(2,1)}, u32[]{:S(2)}) %copy-start.1) | copy-done | bytes 1572888
  4.9 0.0 copy-start.2
  4.9 1.2 %copy-done.2 = bf16[1024,512]{1,0:T(8,128)(2,1)S(1)} copy-done((bf16[1024,512]{1,0:T(8,128)(2,1)S(1)}, bf16[1024,512]{1,0:T(8,128)(2,1)}, u32[]{:S(2)}) %copy-start.2) | copy-done | bytes 1048600
  6.1 0.0 copy-start.3
  6.1 1.0 %copy-done.3 = bf16[1,256,1024]{2,1,0:T(8,128)(2,1)S(1)} copy-done((bf16[1,256,1024]{2,1,0:T(8,128)(2,1)S(1)}, bf16[1,256,1024]{2,1,0:T(8,128)(2,1)}, u32[]{:S(2)}) %copy-start.3) | copy-done | bytes 524312
  7.1 0.0 copy-start.4
  7.1 1.0 %copy-done.4 = bf16[512,512]{1,0:T(8,128)(2,1)S(1)} copy-done((bf16[512,512]{1,0:T(8,128)(2,1)S(1)}, bf16[512,512]{1,0:T(8,128)(2,1)}, u32[]{:S(2)}) %copy-start.4) | copy-done | bytes 524312
  8.2 0.0 copy-start.5
  8.2 0.9 %copy-done.5 = bf16[256,512]{1,0:T(8,128)(2,1)S(1)} copy-done((bf16[256,512]{1,0:T(8,128)(2,1)S(1)}, bf16[256,512]{1,0:T(8,128)(2,1)}, u32[]{:S(2)}) %copy-start.5) | copy-done | bytes 262168
  9.1 0.0 copy-start.6
  9.1 0.9 %copy-done.6 = bf16[16,2304]{1,0:T(8,128)(2,1)S(1)} copy-done((bf16[16,2304]{1,0:T(8,128)(2,1)S(1)}, bf16[16,2304]{1,0:T(8,128)(2,1)}, u32[]{:S(2)}) %copy-start.6) | copy-done | bytes 73752
  10.0 0.0 copy-start.7
  10.0 0.7 copy-done.7
  10.7 0.0 copy-start.8
  10.7 0.7 copy-done.8
  11.3 72.8 %volume.1 = bf16[256,512]{1,0:T(8,128)(2,1)S(1)} custom-call(bf16[256,1024]{1,0:T(8,128)(2,1)S(1)} %bitcast.4, s32[1,96]{1,0:T(1,128)S(1)} %bitcast.5, s32[1,12]{1,0:T(1,128)S(1)} %copy-done.8, bf16[256,512]{1,0:T(8,128)(2,1)S(1)} %copy-done.5, bf16[1,512]{1,0:T(2,128)(2,1)S(1)} %broadcast_in_dim.12.mask_token, ...), custom_call_target="tpu_custom_call" | custom-call | flops 3000000000 | bytes 10485760 | tf_op jit(solution)/shard_map/volume/pallas_call | solution.py:460
  84.1 0.7 copy.14
Async XLA Ops:
  2.1 1.4 %copy-start = (bf16[768,1024]{1,0:T(8,128)(2,1)S(1)}, bf16[768,1024]{1,0:T(8,128)(2,1)}, u32[]{:S(2)}) copy-start(bf16[768,1024]{1,0:T(8,128)(2,1)} %enc_wo.1) | copy-start | bytes 4718596
  3.5 1.4 %copy-start.1 = (bf16[512,1536]{1,0:T(8,128)(2,1)S(1)}, bf16[512,1536]{1,0:T(8,128)(2,1)}, u32[]{:S(2)}) copy-start(bf16[512,1536]{1,0:T(8,128)(2,1)} %dec_qkv.1) | copy-start | bytes 4718596
  4.9 1.2 %copy-start.2 = (bf16[1024,512]{1,0:T(8,128)(2,1)S(1)}, bf16[1024,512]{1,0:T(8,128)(2,1)}, u32[]{:S(2)}) copy-start(bf16[1024,512]{1,0:T(8,128)(2,1)} %enc_to_dec.1) | copy-start | bytes 3145732
  6.1 1.0 %copy-start.3 = (bf16[1,256,1024]{2,1,0:T(8,128)(2,1)S(1)}, bf16[1,256,1024]{2,1,0:T(8,128)(2,1)}, u32[]{:S(2)}) copy-start(bf16[1,256,1024]{2,1,0:T(8,128)(2,1)} %param.12) | copy-start | bytes 1572868
  7.1 1.0 %copy-start.4 = (bf16[512,512]{1,0:T(8,128)(2,1)S(1)}, bf16[512,512]{1,0:T(8,128)(2,1)}, u32[]{:S(2)}) copy-start(bf16[512,512]{1,0:T(8,128)(2,1)} %dec_wo.1) | copy-start | bytes 1572868
  8.2 0.9 %copy-start.5 = (bf16[256,512]{1,0:T(8,128)(2,1)S(1)}, bf16[256,512]{1,0:T(8,128)(2,1)}, u32[]{:S(2)}) copy-start(bf16[256,512]{1,0:T(8,128)(2,1)} %pos_embed.1) | copy-start | bytes 786436
  9.1 0.9 %copy-start.6 = (bf16[16,2304]{1,0:T(8,128)(2,1)S(1)}, bf16[16,2304]{1,0:T(8,128)(2,1)}, u32[]{:S(2)}) copy-start(bf16[16,2304]{1,0:T(8,128)(2,1)} %enc_qkv.1) | copy-start | bytes 221188
  10.0 0.7 copy-start.7
  10.7 0.7 copy-start.8

commit v2 on v1

--- a/solution.py
+++ b/solution.py
@@ -77,17 +77,19 @@
     w_all,
     x_all,
     x_own,
-    kv_all,
+    k_all,
     q_all,
-    o_first,
-    m_first,
-    l_first,
+    bias,
+    ewv_t,
+    dwv_t,
     mix_own,
     mix_send,
     mix_recv,
     dn_all,
     dec_in,
-    dkv,
+    dq,
+    dk,
+    dv_t,
     dmix,
     load_sem,
     zs,
@@ -205,9 +207,10 @@
         index = NX - 1 + ((j - 1) * 2 + h) * 2 + (0 if upward else 1)
         remote(cell, cell, ws.at[index], wr.at[index], up if upward else down).wait_recv()
 
-    def wc_copy(offset, of_core):
-        cell = w_all.at[:, (y + offset) % NY, of_core]
-        return remote(cell, cell, cs.at[offset], cr.at[offset], sibling)
+    def wc_copy(offset, h, of_core):
+        cell = w_all.at[pl.ds(h * 2, 2), (y + offset) % NY, of_core]
+        index = offset * 2 + h
+        return remote(cell, cell, cs.at[index], cr.at[index], sibling)
 
     def wx_event():
         for i in range(1, NX):
@@ -216,7 +219,8 @@
         for h in range(2):
             for upward in (True, False):
                 start(wy_copy(1, h, upward))
-        start(wc_copy(0, core))
+        for h in range(2):
+            start(wc_copy(0, h, core))
 
     def wy_event(j, h):
         for upward in (True, False):
@@ -224,10 +228,7 @@
                 wy_recv(j, h, upward)
                 if wy_has(j + 1, h, upward):
                     start(wy_copy(j + 1, h, upward))
-        if h == 1:
-            start(wc_copy(j, core))
-            if j < 4:
-                start(wc_copy(NY - j, core))
+                start(wc_copy(NY - j if upward else j, h, core))
 
     for i in range(3):
         loads["w%d" % i].wait()
@@ -242,7 +243,7 @@
     chosen = jnp.where(chooser, 1.0, 0.0)
     x_vis = dot(jnp.transpose(chosen).astype(BF), patch_v[...])
     x_own[...] = x_vis
-    normed = layer_norm(x_vis, enc_gain[...].astype(F32)).astype(BF)
+    normed = layer_norm(x_vis, enc_gain[...].astype(F32)[None]).astype(BF)
     x_all[OWN] = normed
     for h in range(2):
         for to_right in (True, False):
@@ -252,77 +253,83 @@
     live_chosen = jnp.where(chooser & (slot < count), 1.0, 0.0)
     is_visible = jnp.sum(live_chosen, axis=1, keepdims=True) > 0.5
 
-    key_index = lax.broadcasted_iota(jnp.int32, (1, NZ * CAP), 1)
-    limit = jnp.zeros((1, NZ * CAP), jnp.int32)
+    slot_row = lax.broadcasted_iota(jnp.int32, (CAP, 128), 0)
     for e in range(NZ):
-        limit = jnp.where(
-            key_index >= e * CAP, e * CAP + counts[0, (z + e + NZ - OWN) % NZ], limit
-        )
-    bias = jnp.where(key_index < limit, 0.0, NEGATIVE)
+        alive = slot_row < counts[0, (z + e + NZ - OWN) % NZ]
+        bias[e * CAP : (e + 1) * CAP, :] = jnp.where(alive, 0.0, NEGATIVE)
+    loads["dqkv"].wait()
+    dwv_t[...] = jnp.transpose(dqkv_v[:, 2 * DD :])
 
     wx_event()
     z_event(1, 0)
     wy_event(1, 0)
+    z_event(1, 1)
     wy_event(1, 1)
-    z_event(1, 1)
+    z_event(2, 0)
     wy_event(2, 0)
-    z_event(2, 0)
+    z_event(2, 1)
     wy_event(2, 1)
+    z_event(3, 0)
     wy_event(3, 0)
-    z_event(2, 1)
+    z_event(3, 1)
     wy_event(3, 1)
-    z_event(3, 0)
     wy_event(4, 0)
     wy_event(4, 1)
+    z_event(4, 0)
     for offset in range(NY):
-        wc_copy(offset, 1 - core).wait_recv()
-    z_event(3, 1)
+        for h in range(2):
+            wc_copy(offset, h, 1 - core).wait_recv()
 
     weights = w_all.reshape(D, WG)
 
-    def project(first, last):
+    def project_keys(first, last):
         rows = x_all[first:last].reshape((last - first) * CAP, D)
-        kv_all[first * CAP : last * CAP, :] = dot(rows, weights[:, HG:]).astype(BF)
+        keys = dot(rows, weights[:, HG : 2 * HG]).astype(BF)
+        k_all[first * CAP : last * CAP, :] = keys
+
+    def project_values(first, last):
+        rows = x_all[first:last].reshape((last - first) * CAP, D)
+        return dot_nt(ewv_t[...], rows).astype(BF)
 
     lane = lax.broadcasted_iota(jnp.int32, (2 * CAP, 128), 1) // 64
 
     mate_slot = OWN + 1 - 2 * part
     pair = jnp.concatenate([x_all[mate_slot], x_all[OWN]], axis=0)
-    q_all[...] = (dot(pair, weights[:, :HG]).astype(BF) * 0.125).astype(BF)
-    project(1, 8)
-    z_event(4, 0)
+    queries = (dot(pair, weights[:, :HG]).astype(BF) * 0.125).astype(BF)
+    for p in range(3):
+        two = queries[:, p * 128 : (p + 1) * 128]
+        for s in range(2):
+            one = jnp.where(lane == s, two, jnp.zeros_like(two))
+            q_all[p, s * 2 * CAP : (s + 1) * 2 * CAP, :] = one
+    ewv_t[...] = jnp.transpose(weights[:, 2 * HG :])
+    project_keys(1, 8)
     z_event(4, 1)
-    project(0, 1)
-    project(8, 9)
-
-    def attend(pair_index, first, last):
-        cols = slice(pair_index * 128, (pair_index + 1) * 128)
-        queries = q_all[:, cols]
-        keys = kv_all[first * CAP : last * CAP, cols]
-        values = kv_all[first * CAP : last * CAP, HG + pair_index * 128 : HG + (pair_index + 1) * 128]
-        row_bias = bias[:, first * CAP : last * CAP]
-        parts = []
-        for s in range(2):
-            one = jnp.where(lane == s, queries, jnp.zeros_like(queries))
-            scores = dot_nt(one, keys) + row_bias
-            top = jnp.max(scores, axis=-1, keepdims=True)
-            raised = jnp.exp(scores - top)
-            total = jnp.sum(raised, axis=-1, keepdims=True)
-            parts.append((top, total, dot(raised.astype(BF), values)))
-        (t0, l0, o0), (t1, l1, o1) = parts
-        return (
-            jnp.where(lane == 0, t0, t1),
-            jnp.where(lane == 0, l0, l1),
-            jnp.where(lane == 0, o0, o1),
-        )
+    project_keys(0, 1)
+    project_keys(8, 9)
+
+    def attend(p, first, last, values_t):
+        cols = slice(p * 128, (p + 1) * 128)
+        row_bias = bias[first * CAP : last * CAP, :]
+        scores = dot_nt(k_all[first * CAP : last * CAP, cols], q_all[p])
+        scores = scores + jnp.concatenate([row_bias] * 3, axis=1)
+        top = jnp.max(scores, axis=0, keepdims=True)
+        raised = jnp.exp(scores - top)
+        total = jnp.sum(raised, axis=0, keepdims=True)
+        return top, total, dot(values_t[cols, :], raised.astype(BF))
+
+    state = {}
 
     def first_part(p):
-        cols = slice(p * 128, (p + 1) * 128)
-        top, total, mixed = attend(p, 0, FIRST)
-        m_first[:, cols] = top
-        l_first[:, cols] = total
-        o_first[:, cols] = mixed
-
+        state[p] = attend(p, 0, FIRST, values_first)
+
+    def next_part(p, first, last, values_t):
+        old, old_total, old_mixed = state[p]
+        top, total, mixed = attend(p, first, last, values_t)
+        new = jnp.maximum(old, top)
+        a, b = jnp.exp(old - new), jnp.exp(top - new)
+        state[p] = (new, old_total * a + total * b, old_mixed * a + mixed * b)
+
+    values_first = project_values(0, FIRST)
     first_part(0)
     z_event(5, 0)
     first_part(1)
@@ -330,18 +337,16 @@
     first_part(2)
     z_event(6, 0)
     z_event(6, 1)
-    project(FIRST, NZ)
+    project_keys(FIRST, NZ)
+    values_last = project_values(FIRST, NZ)
     for p in range(3):
+        next_part(p, FIRST, NZ, values_last)
+        _, total, mixed = state[p]
+        turned = jnp.transpose(mixed / total)
+        joined = jnp.where(lane == 0, turned[: 2 * CAP], turned[2 * CAP :]).astype(BF)
         cols = slice(p * 128, (p + 1) * 128)
-        top, total, mixed = attend(p, FIRST, NZ)
-        old = m_first[:, cols]
-        new = jnp.maximum(old, top)
-        a, b = jnp.exp(old - new), jnp.exp(top - new)
-        mixed = o_first[:, cols] * a + mixed * b
-        total = l_first[:, cols] * a + total * b
-        mixed = (mixed / total).astype(BF)
-        mix_send[:, cols] = mixed[:CAP]
-        mix_own[:, cols] = mixed[CAP:]
+        mix_send[:, cols] = joined[:CAP]
+        mix_own[:, cols] = joined[CAP:]
 
     back = remote(mix_send, mix_recv, rs, rr, mate)
     start(back)
@@ -351,15 +356,14 @@
     enc_out = x_own[...] + dot(mix_own[...], wo_v[pl.ds(own_rows, HG), :])
     loads["e2d"].wait()
     loads["pos"].wait()
-    loads["dqkv"].wait()
     loads["dwo"].wait()
     back.wait_recv()
     enc_out = enc_out + dot(mix_recv[...], wo_v[pl.ds(mate_rows, HG), :])
     latent = dot(enc_out.astype(BF), e2d_v[...]).astype(BF)
     placed = dot(live_chosen.astype(BF), latent)
-    dec = jnp.where(is_visible, placed, mask_token[...].astype(F32)) + pos_v[...].astype(F32)
+    dec = jnp.where(is_visible, placed, mask_token[...].astype(F32)[None]) + pos_v[...].astype(F32)
     dec_in[...] = dec
-    dnorm = layer_norm(dec, dec_gain[...].astype(F32)).astype(BF)
+    dnorm = layer_norm(dec, dec_gain[...].astype(F32)[None]).astype(BF)
     dn_all[1] = dnorm[:LAYER]
     dn_all[2] = dnorm[LAYER:]
     halo_r = remote(dn_all.at[2], dn_all.at[0], hs.at[0], hr.at[0], right)
@@ -367,72 +371,59 @@
     start(halo_r)
     start(halo_l)
 
-    proj = dot(dnorm, dqkv_v[...]).astype(BF)
-    dq = proj[:, :DD]
-    dkv[LAYER : LAYER + TOK, :] = proj[:, DD:]
+    proj = dot(dnorm, dqkv_v[:, : 2 * DD]).astype(BF)
+    dk[LAYER : LAYER + TOK, :] = proj[:, DD:]
+    dv_t[:, LAYER : LAYER + TOK] = dot_nt(dwv_t[...], dnorm).astype(BF)
     scale = LOG2E / math.sqrt(DD // DHEADS)
     quad_lane = lax.broadcasted_iota(jnp.int32, (TOK, 128), 1) // 32
-
-    def quad(queries, keys, values, row_bias, lanes):
-        top = total = mixed = None
+    for g in range(4):
+        four = proj[:, g * 128 : (g + 1) * 128]
         for s in range(4):
-            one = jnp.where(lanes == s, queries, jnp.zeros_like(queries))
-            scores = dot_nt(one, keys) * scale
-            if row_bias is not None:
-                scores = scores + row_bias
-            t = jnp.max(scores, axis=-1, keepdims=True)
-            raised = jnp.exp2(scores - t)
-            l = jnp.sum(raised, axis=-1, keepdims=True)
-            o = dot(raised.astype(BF), values)
-            if s == 0:
-                top = jnp.broadcast_to(t, o.shape)
-                total = jnp.broadcast_to(l, o.shape)
-                mixed = o
-            else:
-                top = jnp.where(lanes == s, t, top)
-                total = jnp.where(lanes == s, l, total)
-                mixed = jnp.where(lanes == s, o, mixed)
+            one = jnp.where(quad_lane == s, four, jnp.zeros_like(four))
+            for level in range(2):
+                dq[g, level, s * LAYER : (s + 1) * LAYER, :] = one[level * LAYER : (level + 1) * LAYER]
+
+    def quad(g, level, first, last, off_grid):
+        scores = dot_nt(dk[first:last, g * 128 : (g + 1) * 128], dq[g, level]) * scale
+        if off_grid is not None:
+            scores = scores + off_grid
+        top = jnp.max(scores, axis=0, keepdims=True)
+        raised = jnp.exp2(scores - top)
+        total = jnp.sum(raised, axis=0, keepdims=True)
+        weight = raised.astype(BF)
+        mixed = []
+        for s in range(4):
+            head = (g * 4 + s) * 32
+            mixed.append(dot(dv_t[head : head + 32, first:last], weight[:, s * LAYER : (s + 1) * LAYER]))
         return top, total, mixed
 
-    local = []
+    inner = {}
     for g in range(4):
-        cols = slice(g * 128, (g + 1) * 128)
-        local.append(
-            quad(
-                dq[:, cols],
-                dkv[LAYER : LAYER + TOK, cols],
-                dkv[LAYER : LAYER + TOK, DD + g * 128 : DD + (g + 1) * 128],
-                None,
-                quad_lane,
-            )
-        )
-
+        for level in range(2):
+            inner[g, level] = quad(g, level, LAYER, LAYER + TOK, None)
+
+    edges = ((0, LAYER), (LAYER + TOK, 2 * LAYER + TOK))
     halo_r.wait_recv()
     halo_l.wait_recv()
-    dkv[:LAYER, :] = dot(dn_all[0], dqkv_v[:, DD:]).astype(BF)
-    dkv[LAYER + TOK :, :] = dot(dn_all[3], dqkv_v[:, DD:]).astype(BF)
-    low_bias = jnp.where(z == 0, NEGATIVE, 0.0)
-    high_bias = jnp.where(z == NZ - 1, NEGATIVE, 0.0)
-    half_lane = quad_lane[:LAYER]
+    for level, (first, last) in enumerate(edges):
+        rows = dn_all[3 * level]
+        dk[first:last, :] = dot(rows, dqkv_v[:, DD : 2 * DD]).astype(BF)
+        dv_t[:, first:last] = dot_nt(dwv_t[...], rows).astype(BF)
+    off = (jnp.where(z == 0, NEGATIVE, 0.0), jnp.where(z == NZ - 1, NEGATIVE, 0.0))
     for g in range(4):
-        cols = slice(g * 128, (g + 1) * 128)
-        value_cols = slice(DD + g * 128, DD + (g + 1) * 128)
-        for level in range(2):
-            rows = slice(level * LAYER, (level + 1) * LAYER)
-            key_rows = slice(0, LAYER) if level == 0 else slice(LAYER + TOK, 2 * LAYER + TOK)
-            top, total, mixed = quad(
-                dq[rows, cols],
-                dkv[key_rows, cols],
-                dkv[key_rows, value_cols],
-                low_bias if level == 0 else high_bias,
-                half_lane,
-            )
-            old = local[g][0][rows]
+        for level, (first, last) in enumerate(edges):
+            old, old_total, old_mixed = inner[g, level]
+            top, total, mixed = quad(g, level, first, last, off[level])
             new = jnp.maximum(old, top)
             a, b = jnp.exp2(old - new), jnp.exp2(top - new)
-            mixed = local[g][2][rows] * a + mixed * b
-            total = local[g][1][rows] * a + total * b
-            dmix[rows, cols] = (mixed / total).astype(BF)
+            share = 1.0 / (old_total * a + total * b)
+            a, b = a * share, b * share
+            heads = []
+            for s in range(4):
+                at = slice(s * LAYER, (s + 1) * LAYER)
+                heads.append(old_mixed[s] * a[:, at] + mixed[s] * b[:, at])
+            turned = jnp.transpose(jnp.concatenate(heads, axis=0))
+            dmix[level * LAYER : (level + 1) * LAYER, g * 128 : (g + 1) * 128] = turned.astype(BF)
     out[...] = (dec_in[...] + dot(dmix[...], dwo_v[...])).astype(BF)
 
     for copy in sends:
@@ -472,32 +463,34 @@
             pltpu.VMEM((NX, NY, NC, ROWS, WG), BF),
             pltpu.VMEM((NZ, CAP, D), BF),
             pltpu.VMEM((CAP, D), F32),
-            pltpu.VMEM((NZ * CAP, 2 * HG), BF),
-            pltpu.VMEM((2 * CAP, HG), BF),
-            pltpu.VMEM((2 * CAP, HG), F32),
-            pltpu.VMEM((2 * CAP, HG), F32),
-            pltpu.VMEM((2 * CAP, HG), F32),
+            pltpu.VMEM((NZ * CAP, HG), BF),
+            pltpu.VMEM((3, 4 * CAP, 128), BF),
+            pltpu.VMEM((NZ * CAP, 128), F32),
+            pltpu.VMEM((HG, D), BF),
+            pltpu.VMEM((DD, DD), BF),
             pltpu.VMEM((CAP, HG), BF),
             pltpu.VMEM((CAP, HG), BF),
             pltpu.VMEM((CAP, HG), BF),
             pltpu.VMEM((4, LAYER, DD), BF),
             pltpu.VMEM((TOK, DD), F32),
-            pltpu.VMEM((2 * LAYER + TOK, 2 * DD), BF),
+            pltpu.VMEM((4, 2, 4 * LAYER, 128), BF),
+            pltpu.VMEM((2 * LAYER + TOK, DD), BF),
+            pltpu.VMEM((DD, 2 * LAYER + TOK), BF),
             pltpu.VMEM((TOK, DD), BF),
             dma((9,)),
             dma((24,)),
             dma((24,)),
             dma((NX - 1 + 16,)),
             dma((NX - 1 + 16,)),
-            dma((NY,)),
-            dma((NY,)),
+            dma((2 * NY,)),
+            dma((2 * NY,)),
             dma,
             dma,
             dma((2,)),
             dma((2,)),
         ],
         compiler_params=pltpu.CompilerParams(
-            collective_id=0, has_side_effects=True, vmem_limit_bytes=48 * 2**20
+            collective_id=0, has_side_effects=True, vmem_limit_bytes=60 * 2**20
         ),
         cost_estimate=pl.CostEstimate(
             flops=3 * 10**9, bytes_accessed=10 * 2**20, transcendentals=3 * 10**6
@@ -508,12 +501,12 @@
         visible[0],
         counts,
         pos_embed,
-        mask_token[None],
-        enc_gain[None],
+        mask_token,
+        enc_gain,
         enc_qkv,
         enc_wo,
         enc_to_dec,
-        dec_gain[None],
+        dec_gain,
         dec_qkv,
         dec_wo,
     )

time: 85.3 us -> 66.5 us (0.78)
  the two profiles are of different devices: /device:TPU:8 before, /device:TPU:1 now
where the time goes in v2:
time: 66.5 us; the launch traced here: 66.3 us
  Pallas kernels  64.6 us (97%)
  local copies, waits for them, and re-layouts  1.67 us (3%)
    pallas_call x1, Pallas kernels, local(): pl.pallas_call(kernel, out_shape=jax.ShapeDtypeStruct((TOK, DD), BF), in_...  64.6 us
    unnamed x1, local copies, waits for them, and re-layouts  1.67 us

profile of v2, /device:TPU:1, one launch (start us, length us, event | category | flops | bytes accessed | tf_op | source)
XLA Modules:
  0.0 66.3 jit_solution(11833050326190691134)
XLA Ops:
  0.0 64.6 %volume.1 = bf16[256,512]{1,0:T(8,128)(2,1)} custom-call(bf16[256,1024]{1,0:T(8,128)(2,1)} %bitcast.4, s32[1,96]{1,0:T(1,128)} %bitcast.5, s32[1,12]{1,0:T(1,128)} %counts.1, bf16[256,512]{1,0:T(8,128)(2,1)} %pos_embed.1, bf16[512]{0:T(512)(128)(2,1)} %mask_token.1, bf16[1024]{0:T(1024)(128)(2,1)} %enc_gain.1, bf16[16,2304]{1,0:T(8,128)(2,1)} %enc_qkv.1, ...), custom_call_target="tpu_custom_call" | custom-call | flops 3000000000 | bytes 10485760 | tf_op jit(solution)/shard_map/volume/pallas_call | solution.py:451
  64.6 1.7 %copy.14 = bf16[1,256,512]{2,1,0:T(8,128)(2,1)} copy(bf16[1,256,512]{2,1,0:T(8,128)(2,1)} %bitcast.3) | data formatting | bytes 524288

commit v3 on v2

--- a/solution.py
+++ b/solution.py
@@ -20,6 +20,7 @@
 LAYER = 128
 D = 1024
 HA = 768
+HD = HA // HEADS
 HG = HA // 2
 WG = 3 * HG
 DD = 512
@@ -27,8 +28,10 @@
 HALF = CAP // 2
 EPSILON = 1e-06
 NEGATIVE = -1e30
-OWN = 4
-FIRST = 9
+OFFSETS = (-3, -2, -1, 0, 1, 2, 3, -4, 4, -5, 5, 6)
+OWN = 3
+FIRST = 7
+SECOND = 11
 LOG2E = math.log2(math.e)
 
 
@@ -47,11 +50,11 @@
 
 
 def slot_r(k):
-    return (OWN - k) % NZ
+    return OFFSETS.index(-k) if k < 6 else NZ - 1
 
 
 def slot_l(k):
-    return (OWN + k) % NZ
+    return OFFSETS.index(k)
 
 
 def kernel(
@@ -188,24 +191,19 @@
                 if z_has(k + 1, h, to_right):
                     start(z_copy(k + 1, h, to_right))
 
+
     def wx_copy(i, other):
         cell = w_all.at[other, y, core]
         return remote(cell, cell, ws.at[i - 1], wr.at[i - 1], x_dev[i])
 
-    def wy_copy(j, h, upward):
-        owner = (y + NY - (j - 1)) % NY if upward else (y + j - 1) % NY
+    def wy_copy(j, h, upward, step):
+        owner = (y + NY - step) % NY if upward else (y + step) % NY
         cell = w_all.at[pl.ds(h * 2, 2), owner, core]
-        index = NX - 1 + ((j - 1) * 2 + h) * 2 + (0 if upward else 1)
+        index = 3 + ((j - 1) * 2 + h) * 2 + (0 if upward else 1)
         return remote(cell, cell, ws.at[index], wr.at[index], up if upward else down)
 
     def wy_has(j, h, upward):
         return j < 4 or (j == 4 and (h == 0) == upward)
-
-    def wy_recv(j, h, upward):
-        owner = (y + NY - j) % NY if upward else (y + j) % NY
-        cell = w_all.at[pl.ds(h * 2, 2), owner, core]
-        index = NX - 1 + ((j - 1) * 2 + h) * 2 + (0 if upward else 1)
-        remote(cell, cell, ws.at[index], wr.at[index], up if upward else down).wait_recv()
 
     def wc_copy(offset, h, of_core):
         cell = w_all.at[pl.ds(h * 2, 2), (y + offset) % NY, of_core]
@@ -214,21 +212,25 @@
 
     def wx_event():
         for i in range(1, NX):
-            cell = w_all.at[(x + NX - i) % NX, y, core]
-            remote(cell, cell, ws.at[i - 1], wr.at[i - 1], x_dev[i]).wait_recv()
+            wx_copy(i, (x + NX - i) % NX).wait_recv()
         for h in range(2):
             for upward in (True, False):
-                start(wy_copy(1, h, upward))
+                start(wy_copy(1, h, upward, 0))
         for h in range(2):
             start(wc_copy(0, h, core))
 
     def wy_event(j, h):
         for upward in (True, False):
             if wy_has(j, h, upward):
-                wy_recv(j, h, upward)
+                wy_copy(j, h, upward, j).wait_recv()
                 if wy_has(j + 1, h, upward):
-                    start(wy_copy(j + 1, h, upward))
+                    start(wy_copy(j + 1, h, upward, j))
                 start(wc_copy(NY - j if upward else j, h, core))
+
+    def sibling_event():
+        for offset in range(NY):
+            for h in range(2):
+                wc_copy(offset, h, 1 - core).wait_recv()
 
     for i in range(3):
         loads["w%d" % i].wait()
@@ -255,7 +257,7 @@
 
     slot_row = lax.broadcasted_iota(jnp.int32, (CAP, 128), 0)
     for e in range(NZ):
-        alive = slot_row < counts[0, (z + e + NZ - OWN) % NZ]
+        alive = slot_row < counts[0, (z + OFFSETS[e] + NZ) % NZ]
         bias[e * CAP : (e + 1) * CAP, :] = jnp.where(alive, 0.0, NEGATIVE)
     loads["dqkv"].wait()
     dwv_t[...] = jnp.transpose(dqkv_v[:, 2 * DD :])
@@ -273,12 +275,12 @@
     wy_event(3, 0)
     z_event(3, 1)
     wy_event(3, 1)
+    z_event(4, 0)
     wy_event(4, 0)
     wy_event(4, 1)
-    z_event(4, 0)
-    for offset in range(NY):
-        for h in range(2):
-            wc_copy(offset, h, 1 - core).wait_recv()
+    z_event(4, 1)
+    sibling_event()
+    z_event(5, 0)
 
     weights = w_all.reshape(D, WG)
 
@@ -295,17 +297,14 @@
 
     mate_slot = OWN + 1 - 2 * part
     pair = jnp.concatenate([x_all[mate_slot], x_all[OWN]], axis=0)
-    queries = (dot(pair, weights[:, :HG]).astype(BF) * 0.125).astype(BF)
+    queries = (dot(pair, weights[:, :HG]) * (LOG2E / math.sqrt(HD))).astype(BF)
     for p in range(3):
         two = queries[:, p * 128 : (p + 1) * 128]
         for s in range(2):
             one = jnp.where(lane == s, two, jnp.zeros_like(two))
             q_all[p, s * 2 * CAP : (s + 1) * 2 * CAP, :] = one
     ewv_t[...] = jnp.transpose(weights[:, 2 * HG :])
-    project_keys(1, 8)
-    z_event(4, 1)
-    project_keys(0, 1)
-    project_keys(8, 9)
+    project_keys(0, FIRST)
 
     def attend(p, first, last, values_t):
         cols = slice(p * 128, (p + 1) * 128)
@@ -313,7 +312,7 @@
         scores = dot_nt(k_all[first * CAP : last * CAP, cols], q_all[p])
         scores = scores + jnp.concatenate([row_bias] * 3, axis=1)
         top = jnp.max(scores, axis=0, keepdims=True)
-        raised = jnp.exp(scores - top)
+        raised = jnp.exp2(scores - top)
         total = jnp.sum(raised, axis=0, keepdims=True)
         return top, total, dot(values_t[cols, :], raised.astype(BF))
 
@@ -326,21 +325,23 @@
         old, old_total, old_mixed = state[p]
         top, total, mixed = attend(p, first, last, values_t)
         new = jnp.maximum(old, top)
-        a, b = jnp.exp(old - new), jnp.exp(top - new)
+        a, b = jnp.exp2(old - new), jnp.exp2(top - new)
         state[p] = (new, old_total * a + total * b, old_mixed * a + mixed * b)
 
+    z_event(5, 1)
     values_first = project_values(0, FIRST)
-    first_part(0)
-    z_event(5, 0)
-    first_part(1)
-    z_event(5, 1)
-    first_part(2)
+    for p in range(3):
+        first_part(p)
+    project_keys(FIRST, SECOND)
+    values_second = project_values(FIRST, SECOND)
+    for p in range(3):
+        next_part(p, FIRST, SECOND, values_second)
     z_event(6, 0)
     z_event(6, 1)
-    project_keys(FIRST, NZ)
-    values_last = project_values(FIRST, NZ)
+    project_keys(SECOND, NZ)
+    values_last = project_values(SECOND, NZ)
     for p in range(3):
-        next_part(p, FIRST, NZ, values_last)
+        next_part(p, SECOND, NZ, values_last)
         _, total, mixed = state[p]
         turned = jnp.transpose(mixed / total)
         joined = jnp.where(lane == 0, turned[: 2 * CAP], turned[2 * CAP :]).astype(BF)
@@ -349,6 +350,7 @@
         mix_own[:, cols] = joined[CAP:]
 
     back = remote(mix_send, mix_recv, rs, rr, mate)
+    early = list(sends)
     start(back)
     loads["wo"].wait()
     own_rows = pl.multiple_of(part * HG, 128)
@@ -357,6 +359,8 @@
     loads["e2d"].wait()
     loads["pos"].wait()
     loads["dwo"].wait()
+    for copy in early:
+        copy.wait_send()
     back.wait_recv()
     enc_out = enc_out + dot(mix_recv[...], wo_v[pl.ds(mate_rows, HG), :])
     latent = dot(enc_out.astype(BF), e2d_v[...]).astype(BF)
@@ -371,10 +375,10 @@
     start(halo_r)
     start(halo_l)
 
-    proj = dot(dnorm, dqkv_v[:, : 2 * DD]).astype(BF)
-    dk[LAYER : LAYER + TOK, :] = proj[:, DD:]
+    scale = LOG2E / math.sqrt(DD // DHEADS)
+    proj = (dot(dnorm, dqkv_v[:, :DD]) * scale).astype(BF)
+    dk[LAYER : LAYER + TOK, :] = dot(dnorm, dqkv_v[:, DD : 2 * DD]).astype(BF)
     dv_t[:, LAYER : LAYER + TOK] = dot_nt(dwv_t[...], dnorm).astype(BF)
-    scale = LOG2E / math.sqrt(DD // DHEADS)
     quad_lane = lax.broadcasted_iota(jnp.int32, (TOK, 128), 1) // 32
     for g in range(4):
         four = proj[:, g * 128 : (g + 1) * 128]
@@ -384,17 +388,15 @@
                 dq[g, level, s * LAYER : (s + 1) * LAYER, :] = one[level * LAYER : (level + 1) * LAYER]
 
     def quad(g, level, first, last, off_grid):
-        scores = dot_nt(dk[first:last, g * 128 : (g + 1) * 128], dq[g, level]) * scale
+        scores = dot_nt(dk[first:last, g * 128 : (g + 1) * 128], dq[g, level])
         if off_grid is not None:
             scores = scores + off_grid
         top = jnp.max(scores, axis=0, keepdims=True)
         raised = jnp.exp2(scores - top)
         total = jnp.sum(raised, axis=0, keepdims=True)
         weight = raised.astype(BF)
-        mixed = []
-        for s in range(4):
-            head = (g * 4 + s) * 32
-            mixed.append(dot(dv_t[head : head + 32, first:last], weight[:, s * LAYER : (s + 1) * LAYER]))
+        wide = dot(dv_t[g * 128 : (g + 1) * 128, first:last], weight)
+        mixed = [wide[s * 32 : (s + 1) * 32, s * LAYER : (s + 1) * LAYER] for s in range(4)]
         return top, total, mixed
 
     inner = {}
@@ -426,7 +428,7 @@
             dmix[level * LAYER : (level + 1) * LAYER, g * 128 : (g + 1) * 128] = turned.astype(BF)
     out[...] = (dec_in[...] + dot(dmix[...], dwo_v[...])).astype(BF)
 
-    for copy in sends:
+    for copy in sends[len(early) :]:
         copy.wait_send()
 
 
@@ -480,8 +482,8 @@
             dma((9,)),
             dma((24,)),
             dma((24,)),
-            dma((NX - 1 + 16,)),
-            dma((NX - 1 + 16,)),
+            dma((19,)),
+            dma((19,)),
             dma((2 * NY,)),
             dma((2 * NY,)),
             dma,

time: 66.5 us -> 64.6 us (0.971)
  the two profiles are of different devices: /device:TPU:1 before, /device:TPU:16 now
where the time goes in v3:
time: 64.6 us; the launch traced here: 64.4 us
  Pallas kernels  62.7 us (97%)
  local copies, waits for them, and re-layouts  1.67 us (3%)
    pallas_call x1, Pallas kernels, local(): pl.pallas_call(kernel, out_shape=jax.ShapeDtypeStruct((TOK, DD), BF), in_...  62.7 us
    unnamed x1, local copies, waits for them, and re-layouts  1.67 us

profile of v3, /device:TPU:16, one launch (start us, length us, event | category | flops | bytes accessed | tf_op | source)
XLA Modules:
  0.0 64.4 jit_solution(1604349424951132909)
XLA Ops:
  0.0 62.7 %volume.1 = bf16[256,512]{1,0:T(8,128)(2,1)} custom-call(bf16[256,1024]{1,0:T(8,128)(2,1)} %bitcast.4, s32[1,96]{1,0:T(1,128)} %bitcast.5, s32[1,12]{1,0:T(1,128)} %counts.1, bf16[256,512]{1,0:T(8,128)(2,1)} %pos_embed.1, bf16[512]{0:T(512)(128)(2,1)} %mask_token.1, bf16[1024]{0:T(1024)(128)(2,1)} %enc_gain.1, bf16[16,2304]{1,0:T(8,128)(2,1)} %enc_qkv.1, ...), custom_call_target="tpu_custom_call" | custom-call | flops 3000000000 | bytes 10485760 | tf_op jit(solution)/shard_map/volume/pallas_call | solution.py:453
  62.7 1.7 %copy.14 = bf16[1,256,512]{2,1,0:T(8,128)(2,1)} copy(bf16[1,256,512]{2,1,0:T(8,128)(2,1)} %bitcast.3) | data formatting | bytes 524288

commit v4 on v3

--- a/solution.py
+++ b/solution.py
@@ -205,10 +205,9 @@
     def wy_has(j, h, upward):
         return j < 4 or (j == 4 and (h == 0) == upward)
 
-    def wc_copy(offset, h, of_core):
-        cell = w_all.at[pl.ds(h * 2, 2), (y + offset) % NY, of_core]
-        index = offset * 2 + h
-        return remote(cell, cell, cs.at[index], cr.at[index], sibling)
+    def wc_copy(offset, of_core):
+        cell = w_all.at[:, (y + offset) % NY, of_core]
+        return remote(cell, cell, cs.at[offset], cr.at[offset], sibling)
 
     def wx_event():
         for i in range(1, NX):
@@ -216,8 +215,7 @@
         for h in range(2):
             for upward in (True, False):
                 start(wy_copy(1, h, upward, 0))
-        for h in range(2):
-            start(wc_copy(0, h, core))
+        start(wc_copy(0, core))
 
     def wy_event(j, h):
         for upward in (True, False):
@@ -225,12 +223,12 @@
                 wy_copy(j, h, upward, j).wait_recv()
                 if wy_has(j + 1, h, upward):
                     start(wy_copy(j + 1, h, upward, j))
-                start(wc_copy(NY - j if upward else j, h, core))
+                if h == 1:
+                    start(wc_copy(NY - j if upward and j < 4 else j, core))
 
     def sibling_event():
         for offset in range(NY):
-            for h in range(2):
-                wc_copy(offset, h, 1 - core).wait_recv()
+            wc_copy(offset, 1 - core).wait_recv()
 
     for i in range(3):
         loads["w%d" % i].wait()
@@ -340,18 +338,20 @@
     z_event(6, 1)
     project_keys(SECOND, NZ)
     values_last = project_values(SECOND, NZ)
+    early = list(sends)
+    back = []
     for p in range(3):
         next_part(p, SECOND, NZ, values_last)
         _, total, mixed = state[p]
         turned = jnp.transpose(mixed / total)
         joined = jnp.where(lane == 0, turned[: 2 * CAP], turned[2 * CAP :]).astype(BF)
         cols = slice(p * 128, (p + 1) * 128)
-        mix_send[:, cols] = joined[:CAP]
+        mix_send[p] = joined[:CAP]
         mix_own[:, cols] = joined[CAP:]
-
-    back = remote(mix_send, mix_recv, rs, rr, mate)
-    early = list(sends)
-    start(back)
+        back.append(remote(mix_send.at[p], mix_recv.at[p], rs.at[p], rr.at[p], mate))
+        back[p].start()
+
+    sends.extend(back)
     loads["wo"].wait()
     own_rows = pl.multiple_of(part * HG, 128)
     mate_rows = pl.multiple_of((1 - part) * HG, 128)
@@ -361,8 +361,10 @@
     loads["dwo"].wait()
     for copy in early:
         copy.wait_send()
-    back.wait_recv()
-    enc_out = enc_out + dot(mix_recv[...], wo_v[pl.ds(mate_rows, HG), :])
+    for copy in back:
+        copy.wait_recv()
+    mix_mate = jnp.concatenate([mix_recv[p] for p in range(3)], axis=1)
+    enc_out = enc_out + dot(mix_mate, wo_v[pl.ds(mate_rows, HG), :])
     latent = dot(enc_out.astype(BF), e2d_v[...]).astype(BF)
     placed = dot(live_chosen.astype(BF), latent)
     dec = jnp.where(is_visible, placed, mask_token[...].astype(F32)[None]) + pos_v[...].astype(F32)
@@ -471,8 +473,8 @@
             pltpu.VMEM((HG, D), BF),
             pltpu.VMEM((DD, DD), BF),
             pltpu.VMEM((CAP, HG), BF),
-            pltpu.VMEM((CAP, HG), BF),
-            pltpu.VMEM((CAP, HG), BF),
+            pltpu.VMEM((3, CAP, 128), BF),
+            pltpu.VMEM((3, CAP, 128), BF),
             pltpu.VMEM((4, LAYER, DD), BF),
             pltpu.VMEM((TOK, DD), F32),
             pltpu.VMEM((4, 2, 4 * LAYER, 128), BF),
@@ -484,10 +486,10 @@
             dma((24,)),
             dma((19,)),
             dma((19,)),
-            dma((2 * NY,)),
-            dma((2 * NY,)),
-            dma,
-            dma,
+            dma((NY,)),
+            dma((NY,)),
+            dma((3,)),
+            dma((3,)),
             dma((2,)),
             dma((2,)),
         ],

time: 64.6 us -> 64.1 us (level)
  the two profiles are of different devices: /device:TPU:16 before, /device:TPU:8 now
where the time goes in v4:
time: 64.1 us; the launch traced here: 63.9 us
  Pallas kernels  62.3 us (97%)
  local copies, waits for them, and re-layouts  1.67 us (3%)
    pallas_call x1, Pallas kernels, local(): pl.pallas_call(kernel, out_shape=jax.ShapeDtypeStruct((TOK, DD), BF), in_...  62.3 us
    unnamed x1, local copies, waits for them, and re-layouts  1.67 us

profile of v4, /device:TPU:8, one launch (start us, length us, event | category | flops | bytes accessed | tf_op | source)
XLA Modules:
  0.0 63.9 jit_solution(15706315426762249773)
XLA Ops:
  0.0 62.3 %volume.1 = bf16[256,512]{1,0:T(8,128)(2,1)} custom-call(bf16[256,1024]{1,0:T(8,128)(2,1)} %bitcast.4, s32[1,96]{1,0:T(1,128)} %bitcast.5, s32[1,12]{1,0:T(1,128)} %counts.1, bf16[256,512]{1,0:T(8,128)(2,1)} %pos_embed.1, bf16[512]{0:T(512)(128)(2,1)} %mask_token.1, bf16[1024]{0:T(1024)(128)(2,1)} %enc_gain.1, bf16[16,2304]{1,0:T(8,128)(2,1)} %enc_qkv.1, ...), custom_call_target="tpu_custom_call" | custom-call | flops 3000000000 | bytes 10485760 | tf_op jit(solution)/shard_map/volume/pallas_call | solution.py:455
  62.3 1.7 %copy.14 = bf16[1,256,512]{2,1,0:T(8,128)(2,1)} copy(bf16[1,256,512]{2,1,0:T(8,128)(2,1)} %bitcast.3) | data formatting | bytes 524288
